TPU v7x, 32 devices: a whole 2x2x4 slice. The times are simulated.
32 devices in a mesh: groups: 2 (over y), oeig: 4 (over z), ieig: 4 (over x, core).
Axes of the slice: x: 2, y: 2, z: 4, core: 2. Of those that a mesh axis runs over, the one named last changes fastest.
Arguments:
- activations: bfloat16 [1536, 8192], P(('groups', 'ieig'), 'oeig'), parts along dimension 0, may hold values from -6 to 6
- out_grads: bfloat16 [1536, 16384], P(('groups', 'oeig'), 'ieig'), parts along dimension 0, may hold values from -6 to 6
- in_basis: bfloat16 [8192, 8192], P('oeig', 'ieig'), may hold values from -0.0625 to 0.0625
- out_basis: bfloat16 [16384, 16384], P('ieig', 'oeig'), may hold values from -0.046875 to 0.046875
- eigenvalues: bfloat16 [16384, 8192], P('oeig', 'ieig'), may hold values from 0.0099487305 to 10
- query_grads: bfloat16 [2, 16384, 8192], P(None, 'oeig', 'ieig'), may hold values from -6 to 6
- seq_lang: int32 [48], P('groups'), parts along dimension 0, may hold values from 0 to 7, as said below
- query_lang: int32 [2], replicated, may hold values from 0 to 7, as said below
Outputs:
- influence: float32 [1536, 2], P(('groups', 'oeig', 'ieig')), parts along dimension 0
There are 2 independent parts, one for each index of `groups`. A program takes and returns all parts, laid end to end along the dimension named above; an argument that names none is the same for every part. Nothing has to cross between parts.
Inputs may be any that keep to these rules, and one draw needn't show every extreme that they name: `seq_lang`: every language occurs among the sequences of a slab. `query_lang`: the queries have different languages, and one of them has language 8 - 1.
All inputs are finite; a program needn't handle non-finite values.
Results may differ from a plain program's by a relative error of at most 0.018.
Values may be sent and summed in bfloat16 or wider, within the bound.
A program may use at most 320 MiB of HBM per device.

v0:
```python
import math

import jax
import jax.numpy as jnp
from jax import lax
from jax.sharding import PartitionSpec as P

OUT = 16384
IN = 8192
SEQ = 32


DAMPING = 0.1


def local(
    activations, out_grads, in_basis, out_basis, eigenvalues, query_grads, seq_lang, query_lang
):
    partial_out = jnp.dot(
        lax.all_gather(out_grads, "oeig", axis=0, tiled=True),
        out_basis,
        preferred_element_type=jnp.float32,
    )
    rotated_out = lax.psum(partial_out.astype(jnp.bfloat16), "ieig")
    partial_in = jnp.dot(
        lax.all_gather(activations, "ieig", axis=0, tiled=True),
        in_basis,
        preferred_element_type=jnp.float32,
    )
    rotated_in = lax.psum(partial_in.astype(jnp.bfloat16), "oeig")
    damped = (query_grads.astype(jnp.float32) / (eigenvalues.astype(jnp.float32) + DAMPING)).astype(
        jnp.bfloat16
    )
    contracted = jnp.einsum("ti,moi->mto", rotated_in, damped, preferred_element_type=jnp.float32)
    partial_score = jnp.sum(contracted * rotated_out.astype(jnp.float32)[None], axis=2).T
    row_count = partial_score.shape[0] // lax.axis_size(("oeig", "ieig"))
    first_row = lax.axis_index(("oeig", "ieig")) * row_count
    summed = lax.psum(partial_score, ("oeig", "ieig"))
    own_rows = lax.dynamic_slice_in_dim(summed, first_row, row_count, 0)
    seq_index = (first_row + jnp.arange(row_count, dtype=jnp.int32)) // SEQ
    onehot = seq_index[:, None] == jnp.arange(seq_lang.shape[0], dtype=jnp.int32)[None, :]
    row_lang = jnp.sum(jnp.where(onehot, seq_lang[None, :], 0), axis=1)
    matched = row_lang[:, None] == query_lang[None, :]
    factor = jnp.where(matched, 1.0, 0.5).astype(jnp.float32)
    return own_rows * (1.0 / math.sqrt(OUT * IN)) * factor


def solution(mesh):
    return jax.shard_map(
        local,
        mesh=mesh,
        in_specs=(
            P(("groups", "ieig"), "oeig"),
            P(("groups", "oeig"), "ieig"),
            P("oeig", "ieig"),
            P("ieig", "oeig"),
            P("oeig", "ieig"),
            P(None, "oeig", "ieig"),
            P("groups"),
            P(),
        ),
        out_specs=P(("groups", "oeig", "ieig"), None),
        check_vma=False,
    )
```

profile of v0, /device:TPU:0, one launch (start us, length us, event | category | flops | bytes accessed | tf_op | source)
XLA Modules:
  0.0 476.3 jit_solution(2329789773900855760)
XLA Ops:
  6.5 0.0 all-gather.5.cloned.1.call-start
  6.5 0.7 all-gather.5.cloned.1.call-update
  7.3 0.0 all-gather.3.cloned.1.call-start
  7.3 0.7 all-gather.3.cloned.1.call-update
  8.0 0.0 all-reduce.5.cloned.1.call-start
  8.1 119.0 %all-gather.5.cloned.1.call-done = bf16[768,4096]{1,0:T(8,128)(2,1)} async-done(((bf16[192,4096]{1,0:T(8,128)(2,1)}), bf16[768,4096]{1,0:T(8,128)(2,1)}) %all-gather.5.cloned.1.call-update) | async-done | bytes 6291472 | tf_op jit(solution)/shard_map/all_gather | solution.py:20
  127.0 33.0 %convolution_convert_fusion = bf16[768,4096]{1,0:T(8,128)(2,1)} fusion(bf16[768,4096]{1,0:T(8,128)(2,1)} %all-gather.5.cloned.1.call-done, bf16[4096,4096]{1,0:T(8,128)(2,1)} %param.11), kind=kOutput, calls=%fused_computation.5 | convolution fusion | flops 25772949504 | bytes 46137344 | tf_op jit(solution)/shard_map/dot_general | solution.py:19
  160.0 0.0 all-reduce.5.cloned.1.call-update
  160.0 0.2 all-reduce.3.cloned.1.call-start
  160.3 0.0 copy-start.1
  160.3 0.0 all-gather.3.cloned.1.call-done
  160.3 12.3 %convolution_convert_fusion.1 = bf16[768,2048]{1,0:T(8,128)(2,1)} fusion(bf16[768,2048]{1,0:T(8,128)(2,1)} %all-gather.3.cloned.1.call-done, bf16[2048,2048]{1,0:T(8,128)(2,1)} %param.10), kind=kOutput, calls=%fused_computation.6 | convolution fusion | flops 6444023808 | bytes 14680064 | tf_op jit(solution)/shard_map/dot_general | solution.py:25
  172.7 0.0 all-reduce.3.cloned.1.call-update
  172.7 0.0 copy-done.1
  172.7 0.1 select_reduce_fusion
  172.8 18.9 %convert_add_fusion = f32[4096,2048]{1,0:T(8,128)} fusion(bf16[4096,2048]{1,0:T(8,128)(2,1)} %param.12), kind=kLoop, calls=%fused_computation.1 | loop fusion | flops 16777216 | bytes 50331648 | tf_op jit(solution)/shard_map/add | solution.py:31
  191.7 86.3 %all-reduce.5.cloned.1.call-done = bf16[768,4096]{1,0:T(8,128)(2,1)} async-done(((bf16[768,4096]{1,0:T(8,128)(2,1)}), bf16[768,4096]{1,0:T(8,128)(2,1)}) %all-reduce.5.cloned.1.call-update) | async-done | bytes 6291472 | tf_op jit(solution)/shard_map/psum | solution.py:24
  278.0 9.5 %copy.10 = f32[768,4096]{0,1:T(8,128)} copy(bf16[768,4096]{1,0:T(8,128)(2,1)} %all-reduce.5.cloned.1.call-done) | data formatting | bytes 18874368 | tf_op jit(solution)/shard_map/convert_element_type | solution.py:35
  287.5 0.0 copy-start
  287.5 114.1 %all-reduce.3.cloned.1.call-done = bf16[768,2048]{1,0:T(8,128)(2,1)} async-done(((bf16[768,2048]{1,0:T(8,128)(2,1)}), bf16[768,2048]{1,0:T(8,128)(2,1)}) %all-reduce.3.cloned.1.call-update) | async-done | bytes 3145744 | tf_op jit(solution)/shard_map/psum | solution.py:30
  401.6 35.7 %fusion.1 = f32[2,768]{1,0:T(2,128)S(1)} fusion(f32[768,4096]{0,1:T(8,128)} %copy.10, bf16[2,4096,2048]{2,1,0:T(8,128)(2,1)} %param.13, f32[4096,2048]{1,0:T(8,128)} %convert_add_fusion, bf16[768,2048]{1,0:T(8,128)(2,1)} %all-reduce.3.cloned.1.call-done), kind=kOutput, calls=%fused_computation.4 | convolution fusion | flops 25832716288 | bytes 82843648 | tf_op jit(solution)/shard_map/ti,moi->mto/dot_general | solution.py:34
  437.2 31.9 %psum.23 = f32[768,2]{0,1:T(2,128)S(1)} all-reduce(f32[768,2]{0,1:T(2,128)S(1)} %bitcast.12), channel_id=1, replica_groups=mesh['groups'=2,'oeig'=4,'ieig'=4] {'oeig','ieig'}, use_global_device_ids=true, to_apply=%region_3.0 | all-reduce | flops 1536 | bytes 12288 | tf_op jit(solution)/shard_map/psum | solution.py:38
  469.1 0.0 copy-done
  469.1 0.6 fusion.3
  (1 shorter events, 0.0 us)
Async XLA Ops:
  6.5 120.5 %all-gather.5.cloned.1.call-start = ((), (), s32[]{:S(2)}) async-start(), calls=%async_computation.2 | async-start | bytes 7864320 | tf_op jit(solution)/shard_map/all_gather | solution.py:20
  7.3 153.1 %all-gather.3.cloned.1.call-start = ((), (), s32[]{:S(2)}) async-start(), calls=%async_computation | async-start | bytes 3932160 | tf_op jit(solution)/shard_map/all_gather | solution.py:26
  8.0 270.0 %all-reduce.5.cloned.1.call-start = ((), (), s32[]{:S(2)}) async-start(), calls=%async_computation.3 | async-start | bytes 12582912 | tf_op jit(solution)/shard_map/psum | solution.py:24
  160.0 241.5 %all-reduce.3.cloned.1.call-start = ((), (), s32[]{:S(2)}) async-start(), calls=%async_computation.1 | async-start | bytes 6291456 | tf_op jit(solution)/shard_map/psum | solution.py:30
  160.3 12.4 %copy-start.1 = (s32[24]{0:T(128)S(1)}, s32[24]{0:T(128)}, u32[]{:S(2)}) copy-start(s32[24]{0:T(128)} %param.14) | copy-start | bytes 292
  287.5 181.6 %copy-start = (s32[2]{0:T(128)S(1)}, s32[2]{0:T(128)}, u32[]{:S(2)}) copy-start(s32[2]{0:T(128)} %param.15) | copy-start | bytes 28
Sparse Core Ops, SparseCore 0:
  8.9 118.0 all-gather.4
  128.6 26.7 all-gather.2
  160.2 117.7 all-reduce.4
  280.2 121.2 all-reduce.2
where the time goes:
time: 477 us; the launch traced here: 476 us
  waiting for transfers between devices  321 us (67%)
  matrix products  81 us (17%)
  blocking collectives  31.9 us (7%)
  other arithmetic  19.6 us (4%)
  between operations  13.2 us (3%)
  local copies, waits for them, and re-layouts  9.5 us (2%)
    all_gather x1, waiting for transfers between devices, local(): lax.all_gather(out_grads, 'oeig', axis=0, tiled=True)  119 us
    psum x1, waiting for transfers between devices, local(): rotated_in = lax.psum(partial_in.astype(jnp.bfloat16), 'oeig')  114 us
    psum x1, waiting for transfers between devices, local(): rotated_out = lax.psum(partial_out.astype(jnp.bfloat16), 'ieig')  86.3 us
    dot_general x1, matrix products, local(): jnp.einsum('ti,moi->mto', rotated_in, damped, preferred_element_type=jnp....  35.7 us
    dot_general x1, matrix products, local(): jnp.dot(lax.all_gather(out_grads, 'oeig', axis=0, tiled=True), out_basis,...  33 us
    psum x1, blocking collectives, local(): summed = lax.psum(partial_score, ('oeig', 'ieig'))  31.9 us
    add x1, other arithmetic, local(): eigenvalues.astype(jnp.float32) + DAMPING  18.9 us
    dot_general x1, matrix products, local(): jnp.dot(lax.all_gather(activations, 'ieig', axis=0, tiled=True), in_basis...  12.3 us
  transfers between devices with their start and end apart: 4, of which 3 were waited for; matrix products, arithmetic and copies ran while one was open for 15% of the time, Pallas kernels for 0%

commit v1 on v0

--- a/solution.py
+++ b/solution.py
@@ -1,8 +1,11 @@
+import functools
 import math
 
 import jax
 import jax.numpy as jnp
 from jax import lax
+from jax.experimental import pallas as pl
+from jax.experimental.pallas import tpu as pltpu
 from jax.sharding import PartitionSpec as P
 
 OUT = 16384
@@ -11,11 +14,449 @@
 
 
 DAMPING = 0.1
-
-
-def local(
-    activations, out_grads, in_basis, out_basis, eigenvalues, query_grads, seq_lang, query_lang
+MESH = pl.DeviceIdType.MESH
+F32 = jnp.float32
+BF16 = jnp.bfloat16
+
+SIDE = 4
+PIECES = 2
+TILE = 512
+DROWS = 128
+STRIP = 16
+
+
+def kernel(
+    act_hbm, og_hbm, ib_hbm, ob_hbm, eig_hbm, qg_hbm,
+    out_ref, d_hbm,
+    og, act, rip, prec, srec, ro, crecv, xrecv, frecv, w, wbuf, qbuf, ebuf, dbuf, sc, rsc,
+    lsem, wsem, qsem, esem, dsem,
+    ring_s, ring_r, act_s, act_r, c_s, c_r, x_s, x_r, f_s, f_r, p_s, p_r, s_s, s_r, sc_s, sc_r,
 ):
+    a, b = lax.axis_index("oeig"), lax.axis_index("ieig")
+    me = a * SIDE + b
+    rows = og.shape[1]
+    piece = rows // PIECES
+    chunks = SIDE * PIECES
+    width = og.shape[2]
+    half = width // 2
+    span = act.shape[2]
+    queries = d_hbm.shape[0]
+    core = lax.rem(b, 2)
+    mate = b + 1 - 2 * core
+    across = lax.rem(b + 2, SIDE)
+    ring_next = lax.rem(2 * a + 1, 5)
+
+    def ring_prev(i):
+        return lax.rem(3 * i + 2, 5)
+
+    owner = [a]
+    for _ in range(SIDE - 1):
+        owner.append(ring_prev(owner[-1]))
+    act_owner = [b, mate, across, lax.rem(mate + 2, SIDE)]
+
+    def remote(src, dst, send, recv, to_a, to_b):
+        return pltpu.make_async_remote_copy(
+            src_ref=src, dst_ref=dst, send_sem=send, recv_sem=recv,
+            device_id={"oeig": to_a, "ieig": to_b}, device_id_type=MESH,
+        )
+
+    barrier = pltpu.get_barrier_semaphore()
+    others = SIDE * SIDE - 1
+
+    @pl.loop(1, others + 1)
+    def _(k):
+        peer = lax.rem(me + k, SIDE * SIDE)
+        pl.semaphore_signal(
+            barrier, inc=1, device_id={"oeig": peer // SIDE, "ieig": lax.rem(peer, SIDE)},
+            device_id_type=MESH,
+        )
+
+    own_og = pltpu.make_async_copy(og_hbm, og.at[0], lsem.at[0])
+    own_act = pltpu.make_async_copy(act_hbm, act.at[0], lsem.at[1])
+    own_og.start()
+    own_act.start()
+    pl.semaphore_wait(barrier, others)
+
+    def ring(step):
+        src = og_hbm if step == 1 else og.at[step - 1]
+        return remote(src, og.at[step], ring_s.at[step], ring_r.at[step], ring_next, b)
+
+    act_x = remote(act_hbm, act.at[2], act_s.at[2], act_r.at[2], a, across)
+    act_c = remote(act_hbm, act.at[1], act_s.at[1], act_r.at[1], a, mate)
+    act_f = remote(act.at[2], act.at[3], act_s.at[3], act_r.at[3], a, mate)
+    act_x.start()
+    act_c.start()
+    ring(1).start()
+
+    def stream(count, source, view, compute):
+        def copy(k):
+            slot = lax.rem(k, 2)
+            return pltpu.make_async_copy(source(k), view(slot), wsem.at[slot])
+
+        copy(jnp.int32(0)).start()
+
+        @pl.loop(0, count)
+        def _(k):
+            @pl.when(k + 1 < count)
+            def _():
+                copy(k + 1).start()
+
+            copy(k).wait()
+            compute(k, view(lax.rem(k, 2)))
+
+    def columns(k):
+        return pl.ds(pl.multiple_of(k * TILE, TILE), TILE)
+
+    def strips(count, body):
+        @pl.loop(0, count // STRIP)
+        def _(i):
+            body(pl.ds(pl.multiple_of(i * STRIP, STRIP), STRIP))
+
+    my_half = pl.ds(pl.multiple_of(core * half, half), half)
+    other_half = pl.ds(pl.multiple_of((1 - core) * half, half), half)
+    my_rows, other_rows = my_half, other_half
+
+    def to_mate(s):
+        return remote(ro.at[s, :, other_half], crecv.at[s], c_s.at[s], c_r.at[s], a, mate)
+
+    def to_across(s):
+        return remote(crecv.at[s], xrecv.at[s], x_s.at[s], x_r.at[s], a, across)
+
+    def whole_to_mate(s):
+        return remote(ro.at[s, :, my_half], frecv.at[s], f_s.at[s], f_r.at[s], a, mate)
+
+    def rotate_out(s):
+        def compute(k, tile):
+            part = jnp.dot(og[s], tile[...], preferred_element_type=F32)
+            ro[s, :, columns(k)] = part.astype(BF16)
+
+        stream(width // TILE, lambda k: ob_hbm.at[:, columns(k)], lambda v: wbuf.at[v], compute)
+        to_mate(s).start()
+
+    def sum_cores(s):
+        to_mate(s).wait_recv()
+
+        def body(r):
+            crecv[s, r, :] = (
+                crecv[s, r, :].astype(F32) + ro[s, r, my_half].astype(F32)
+            ).astype(BF16)
+
+        strips(rows, body)
+        to_across(s).start()
+
+    def sum_across(s):
+        to_across(s).wait_recv()
+
+        def body(r):
+            ro[s, r, my_half] = (
+                crecv[s, r, :].astype(F32) + xrecv[s, r, :].astype(F32)
+            ).astype(BF16)
+
+        strips(rows, body)
+        whole_to_mate(s).start()
+
+    def rotate_in():
+        def compute(k, tile):
+            for s in range(SIDE):
+                part = jnp.dot(act[s], tile[...], preferred_element_type=F32).astype(BF16)
+                for h in range(PIECES):
+                    rip[act_owner[s] * PIECES + h, :, columns(k)] = part[
+                        h * piece : (h + 1) * piece
+                    ]
+
+        stream(
+            span // TILE, lambda k: ib_hbm.at[:, columns(k)],
+            lambda v: wbuf.at[v, pl.ds(0, span), :], compute,
+        )
+
+    def damp(first, last):
+        def block(k):
+            return pl.ds(pl.multiple_of(k * DROWS, DROWS), DROWS)
+
+        def loads(k):
+            v = lax.rem(k, 2)
+            return (
+                pltpu.make_async_copy(qg_hbm.at[:, block(k), :], qbuf.at[v], qsem.at[v]),
+                pltpu.make_async_copy(eig_hbm.at[block(k), :], ebuf.at[v], esem.at[v]),
+            )
+
+        def store(k):
+            v = lax.rem(k, 2)
+            return pltpu.make_async_copy(dbuf.at[v], d_hbm.at[:, block(k), :], dsem.at[v])
+
+        for c in loads(jnp.int32(first)):
+            c.start()
+
+        @pl.loop(first, last)
+        def _(k):
+            v = lax.rem(k, 2)
+
+            @pl.when(k + 1 < last)
+            def _():
+                for c in loads(k + 1):
+                    c.start()
+
+            for c in loads(k):
+                c.wait()
+
+            @pl.when(k >= first + 2)
+            def _():
+                store(k - 2).wait()
+
+            def body(r):
+                inv = 1.0 / (ebuf[v, r, :].astype(F32) + DAMPING)
+                for m in range(queries):
+                    dbuf[v, m, r, :] = (qbuf[v, m, r, :].astype(F32) * inv).astype(BF16)
+
+            strips(DROWS, body)
+            store(k).start()
+
+        for k in (last - 2, last - 1):
+            store(jnp.int32(k)).wait()
+
+    tiles = span // TILE
+
+    def contract(s):
+        whole_to_mate(s).wait_recv()
+
+        def compute(k, tile):
+            mine = jnp.dot(ro[s, :, my_half], tile[my_rows, :], preferred_element_type=F32)
+            w[s, :, columns(k)] = mine + jnp.dot(
+                frecv[s], tile[other_rows, :], preferred_element_type=F32
+            )
+
+        stream(
+            queries * tiles,
+            lambda k: d_hbm.at[k // tiles, :, columns(lax.rem(k, tiles))],
+            lambda v: wbuf.at[v], compute,
+        )
+
+    last_a = SIDE - 1
+    up = lax.rem(a + 1, SIDE)
+    down = lax.rem(a + last_a, SIDE)
+
+    def going_up(c):
+        return remote(prec.at[c], prec.at[c], p_s.at[c], p_r.at[c], up, b)
+
+    def outgoing(c):
+        start = pl.multiple_of(lax.rem(c, PIECES) * piece, piece)
+        return act.at[lax.div(c, PIECES), pl.ds(start, piece), :]
+
+    def going_down(c):
+        return remote(outgoing(c), srec.at[c], s_s.at[c], s_r.at[c], down, b)
+
+    def chain(step):
+        c = step - a
+
+        @pl.when((c >= 0) & (c < chunks))
+        def _():
+            @pl.when(a == 0)
+            def _():
+                def body(r):
+                    prec[c, r, :] = rip[c, r, :]
+
+                strips(piece, body)
+
+            @pl.when(a > 0)
+            def _():
+                going_up(c).wait_recv()
+
+                def body(r):
+                    prec[c, r, :] = (
+                        prec[c, r, :].astype(F32) + rip[c, r, :].astype(F32)
+                    ).astype(BF16)
+
+                strips(piece, body)
+
+            @pl.when(a < last_a)
+            def _():
+                going_up(c).start()
+
+        e = step - (last_a - a)
+
+        @pl.when((e >= 0) & (e < chunks))
+        def _():
+            @pl.when(a == last_a)
+            def _():
+                def body(r):
+                    srec[e, r, :] = jnp.zeros_like(srec[e, r, :])
+                    outgoing(e)[r, :] = rip[e, r, :]
+
+                strips(piece, body)
+
+            @pl.when(a < last_a)
+            def _():
+                going_down(e).wait_recv()
+
+                def body(r):
+                    outgoing(e)[r, :] = (
+                        srec[e, r, :].astype(F32) + rip[e, r, :].astype(F32)
+                    ).astype(BF16)
+
+                strips(piece, body)
+
+            @pl.when(a > 0)
+            def _():
+                going_down(e).start()
+
+    dtiles = d_hbm.shape[1] // DROWS
+
+    own_og.wait()
+    rotate_out(0)
+    own_act.wait()
+    act_x.wait_recv()
+    act_f.start()
+    act_c.wait_recv()
+    sum_cores(0)
+    act_f.wait_recv()
+    rotate_in()
+    for c in (act_x, act_c, act_f):
+        c.wait_send()
+    damp(0, dtiles // 2)
+    sum_across(0)
+
+    ring(1).wait_recv()
+    ring(2).start()
+    rotate_out(1)
+    damp(dtiles // 2, dtiles)
+    sum_cores(1)
+
+    ring(2).wait_recv()
+    ring(3).start()
+    chain(0)
+    rotate_out(2)
+    sum_across(1)
+    chain(1)
+    contract(0)
+    sum_cores(2)
+    chain(2)
+    contract(1)
+    sum_across(2)
+    chain(3)
+
+    ring(3).wait_recv()
+    rotate_out(3)
+    chain(4)
+    sum_cores(3)
+    chain(5)
+    contract(2)
+    sum_across(3)
+    chain(6)
+    contract(3)
+    for step in range(7, chunks + last_a):
+        chain(step)
+
+    lane = lax.broadcasted_iota(jnp.int32, (STRIP, sc.shape[2]), 1)
+    per = sc.shape[1]
+    for s in range(SIDE):
+        for h in range(PIECES):
+            c = owner[s] * PIECES + h
+
+            @pl.loop(0, piece // STRIP)
+            def _(i):
+                r = pl.ds(pl.multiple_of(i * STRIP, STRIP), STRIP)
+                total = prec[c, r, :].astype(F32) + srec[c, r, :].astype(F32)
+                wr = pl.ds(pl.multiple_of(h * piece + i * STRIP, STRIP), STRIP)
+                packed = jnp.zeros(lane.shape, F32)
+                for m in range(queries):
+                    got = jnp.sum(
+                        total * w[s, wr, m * span : (m + 1) * span], axis=1, keepdims=True
+                    )
+                    packed = jnp.where(lane == m, got, packed)
+                row = owner[s] * rows + h * piece + i * STRIP
+                sc[row // per, pl.ds(pl.multiple_of(lax.rem(row, per), STRIP), STRIP), :] = packed
+
+    def score(k):
+        peer = lax.rem(me + k, SIDE * SIDE)
+        return remote(
+            sc.at[peer], rsc.at[k], sc_s.at[k], sc_r.at[k], peer // SIDE, lax.rem(peer, SIDE)
+        )
+
+    @pl.loop(1, others + 1)
+    def _(k):
+        score(k).start()
+
+    rsc[0] = sc[me]
+
+    for step in range(1, SIDE):
+        ring(step).wait_send()
+    for s in range(SIDE):
+        to_mate(s).wait_send()
+        to_across(s).wait_send()
+        whole_to_mate(s).wait_send()
+
+    @pl.loop(0, chunks)
+    def _(c):
+        @pl.when(a < last_a)
+        def _():
+            going_up(c).wait_send()
+
+        @pl.when(a > 0)
+        def _():
+            going_down(c).wait_send()
+
+    @pl.loop(1, others + 1)
+    def _(k):
+        score(k).wait()
+
+    total = rsc[0]
+    for k in range(1, SIDE * SIDE):
+        total = total + rsc[k]
+    out_ref[...] = total
+
+
+def fused_scores(activations, out_grads, in_basis, out_basis, eigenvalues, query_grads):
+    rows, span = activations.shape
+    width = out_grads.shape[1]
+    queries = query_grads.shape[0]
+    chunks, piece = SIDE * PIECES, rows // PIECES
+    devices = SIDE * SIDE
+    per = SIDE * rows // devices
+    vmem = pltpu.VMEM
+    dma = pltpu.SemaphoreType.DMA
+    any_space = pl.BlockSpec(memory_space=pl.ANY)
+    out, _ = pl.pallas_call(
+        kernel,
+        out_shape=(
+            jax.ShapeDtypeStruct((per, 128), F32),
+            jax.ShapeDtypeStruct(query_grads.shape, BF16),
+        ),
+        in_specs=[any_space] * 6,
+        out_specs=(pl.BlockSpec(memory_space=pltpu.VMEM), any_space),
+        scratch_shapes=[
+            vmem((SIDE, rows, width), BF16),
+            vmem((SIDE, rows, span), BF16),
+            vmem((chunks, piece, span), BF16),
+            vmem((chunks, piece, span), BF16),
+            vmem((chunks, piece, span), BF16),
+            vmem((SIDE, rows, width), BF16),
+            vmem((SIDE, rows, width // 2), BF16),
+            vmem((SIDE, rows, width // 2), BF16),
+            vmem((SIDE, rows, width // 2), BF16),
+            vmem((SIDE, rows, queries * span), F32),
+            vmem((2, width, TILE), BF16),
+            vmem((2, queries, DROWS, span), BF16),
+            vmem((2, DROWS, span), BF16),
+            vmem((2, queries, DROWS, span), BF16),
+            vmem((devices, per, 128), F32),
+            vmem((devices, per, 128), F32),
+        ]
+        + [dma((2,))] * 5
+        + [dma((SIDE,))] * 10
+        + [dma((chunks,))] * 4
+        + [dma((devices,))] * 2,
+        compiler_params=pltpu.CompilerParams(
+            collective_id=0, has_side_effects=True, vmem_limit_bytes=63 * 1024 * 1024
+        ),
+        cost_estimate=pl.CostEstimate(
+            flops=2 * SIDE * rows * (width * width + span * span + queries * width * span),
+            bytes_accessed=2 * (8 * width * width + span * span), transcendentals=0,
+        ),
+    )(activations, out_grads, in_basis, out_basis, eigenvalues, query_grads)
+    return out[:, :queries]
+
+
+def plain_scores(activations, out_grads, in_basis, out_basis, eigenvalues, query_grads):
     partial_out = jnp.dot(
         lax.all_gather(out_grads, "oeig", axis=0, tiled=True),
         out_basis,
@@ -36,7 +477,17 @@
     row_count = partial_score.shape[0] // lax.axis_size(("oeig", "ieig"))
     first_row = lax.axis_index(("oeig", "ieig")) * row_count
     summed = lax.psum(partial_score, ("oeig", "ieig"))
-    own_rows = lax.dynamic_slice_in_dim(summed, first_row, row_count, 0)
+    return lax.dynamic_slice_in_dim(summed, first_row, row_count, 0)
+
+
+def local(
+    fused, activations, out_grads, in_basis, out_basis, eigenvalues, query_grads, seq_lang,
+    query_lang,
+):
+    scores = fused_scores if fused else plain_scores
+    own_rows = scores(activations, out_grads, in_basis, out_basis, eigenvalues, query_grads)
+    row_count = own_rows.shape[0]
+    first_row = lax.axis_index(("oeig", "ieig")) * row_count
     seq_index = (first_row + jnp.arange(row_count, dtype=jnp.int32)) // SEQ
     onehot = seq_index[:, None] == jnp.arange(seq_lang.shape[0], dtype=jnp.int32)[None, :]
     row_lang = jnp.sum(jnp.where(onehot, seq_lang[None, :], 0), axis=1)
@@ -46,8 +497,9 @@
 
 
 def solution(mesh):
+    fused = mesh.shape["oeig"] == SIDE and mesh.shape["ieig"] == SIDE
     return jax.shard_map(
-        local,
+        functools.partial(local, fused),
         mesh=mesh,
         in_specs=(
             P(("groups", "ieig"), "oeig"),

time: 477 us -> 275 us (0.58)
  waiting for transfers between devices: 321 us -> 0 us
  Pallas kernels: 0 us -> 272 us
  matrix products: 81 us -> 0 us
  blocking collectives: 31.9 us -> 0 us
  other arithmetic: 19.6 us -> 0.91 us
  between operations: 13.2 us -> 0.03 us
  local copies, waits for them, and re-layouts: 9.5 us -> 0.65 us
    pallas_call x0 -> x1, Pallas kernels: none -> 272 us  [fused_scores(): pl.pallas_call(kernel, out_shape=(jax.ShapeDtypeStruct((per, 128), F32),...]
    psum x2 -> x0, waiting for transfers between devices: 200 us -> none  [the longest x1 114 us: local(): rotated_in = lax.psum(partial_in.astype(jnp.bfloat16), 'oeig')]
    all_gather x2 -> x0, waiting for transfers between devices: 119 us -> none  [the longest x1 119 us: local(): lax.all_gather(out_grads, 'oeig', axis=0, tiled=True)]
    dot_general x3 -> x0, matrix products: 81 us -> none  [the longest x1 35.7 us: local(): jnp.einsum('ti,moi->mto', rotated_in, damped, preferred_element_type=jnp....]
    psum x1 -> x0, blocking collectives: 31.9 us -> none  [local(): summed = lax.psum(partial_score, ('oeig', 'ieig'))]
    add x1 -> x0, other arithmetic: 18.9 us -> none  [local(): eigenvalues.astype(jnp.float32) + DAMPING]
    convert_element_type x1 -> x0, local copies, waits for them, and re-layouts: 9.49 us -> none  [local(): rotated_out.astype(jnp.float32)[None]]
  transfers between devices with their start and end apart: 4 -> 0, of which waited for: 3 -> 0; matrix products, arithmetic and copies ran while one was open for 15% -> 0% of each run, Pallas kernels for 0% -> 0%
where the time goes in v1:
time: 275 us; the launch traced here: 274 us
  Pallas kernels  272 us (99%)
    pallas_call x1, Pallas kernels, fused_scores(): pl.pallas_call(kernel, out_shape=(jax.ShapeDtypeStruct((per, 128), F32),...  272 us

profile of v1, /device:TPU:0, one launch (start us, length us, event | category | flops | bytes accessed | tf_op | source)
XLA Modules:
  0.0 273.8 jit_solution(13705633606451111438)
XLA Ops:
  0.0 0.0 copy-start
  0.0 0.0 copy-start.1
  0.0 272.2 %shard_map.82 = (f32[48,128]{1,0:T(8,128)}, bf16[2,4096,2048]{2,1,0:T(8,128)(2,1)}) custom-call(bf16[192,2048]{1,0:T(8,128)(2,1)} %act_hbm.1, bf16[192,4096]{1,0:T(8,128)(2,1)} %og_hbm.1, bf16[2048,2048]{1,0:T(8,128)(2,1)} %ib_hbm.1, bf16[4096,4096]{1,0:T(8,128)(2,1)} %ob_hbm.1, bf16[4096,2048]{1,0:T(8,128)(2,1)} %eig_hbm.1, bf16[2,4096,2048]{2,1,0:T(8,128)(2,1)} %qg_hbm.1), custom_call_target="tpu_custom_call" | custom-call | flops 57982058496 | bytes 276824064 | tf_op jit(solution)/shard_map/pallas_call | solution.py:418
  272.3 0.0 copy-done.1
  272.3 0.1 select_reduce_fusion
  272.4 0.0 copy-done
  272.4 0.8 select_multiply_fusion
  273.2 0.6 copy.12
  (1 shorter events, 0.0 us)
Async XLA Ops:
  0.0 272.4 %copy-start = (s32[2]{0:T(128)S(1)}, s32[2]{0:T(128)}, u32[]{:S(2)}) copy-start(s32[2]{0:T(128)} %param.15) | copy-start | bytes 28
  0.0 272.3 %copy-start.1 = (s32[24]{0:T(128)S(1)}, s32[24]{0:T(128)}, u32[]{:S(2)}) copy-start(s32[24]{0:T(128)} %param.14) | copy-start | bytes 292

commit v2 on v1

--- a/solution.py
+++ b/solution.py
@@ -23,6 +23,11 @@
 TILE = 512
 DROWS = 128
 STRIP = 16
+
+
+def reciprocal(x):
+    guess = pl.reciprocal(x, approx=True)
+    return guess * (2.0 - x * guess)
 
 
 def kernel(
@@ -45,13 +50,6 @@
     mate = b + 1 - 2 * core
     across = lax.rem(b + 2, SIDE)
     ring_next = lax.rem(2 * a + 1, 5)
-
-    def ring_prev(i):
-        return lax.rem(3 * i + 2, 5)
-
-    owner = [a]
-    for _ in range(SIDE - 1):
-        owner.append(ring_prev(owner[-1]))
     act_owner = [b, mate, across, lax.rem(mate + 2, SIDE)]
 
     def remote(src, dst, send, recv, to_a, to_b):
@@ -204,7 +202,7 @@
                 store(k - 2).wait()
 
             def body(r):
-                inv = 1.0 / (ebuf[v, r, :].astype(F32) + DAMPING)
+                inv = reciprocal(ebuf[v, r, :].astype(F32) + DAMPING)
                 for m in range(queries):
                     dbuf[v, m, r, :] = (qbuf[v, m, r, :].astype(F32) * inv).astype(BF16)
 
@@ -216,14 +214,17 @@
 
     tiles = span // TILE
 
-    def contract(s):
-        whole_to_mate(s).wait_recv()
+    def contract(s, count):
+        for k in range(s, s + count):
+            whole_to_mate(k).wait_recv()
+        slots = pl.ds(s, count)
 
         def compute(k, tile):
-            mine = jnp.dot(ro[s, :, my_half], tile[my_rows, :], preferred_element_type=F32)
-            w[s, :, columns(k)] = mine + jnp.dot(
-                frecv[s], tile[other_rows, :], preferred_element_type=F32
-            )
+            mine = ro[slots, :, my_half].reshape(count * rows, half)
+            theirs = frecv[slots].reshape(count * rows, half)
+            got = jnp.dot(mine, tile[my_rows, :], preferred_element_type=F32)
+            got = got + jnp.dot(theirs, tile[other_rows, :], preferred_element_type=F32)
+            w[slots, :, columns(k)] = got.reshape(count, rows, TILE)
 
         stream(
             queries * tiles,
@@ -298,6 +299,49 @@
             @pl.when(a > 0)
             def _():
                 going_down(e).start()
+
+    lane = lax.broadcasted_iota(jnp.int32, (STRIP, sc.shape[2]), 1)
+    per = sc.shape[1]
+    parcels = piece // per
+
+    def place(i):
+        return i + (i // 2) * (1 - 2 * lax.rem(i, 2))
+
+    def score(peer):
+        k = lax.rem(peer - me + SIDE * SIDE, SIDE * SIDE)
+        return k, remote(
+            sc.at[peer], rsc.at[k], sc_s.at[k], sc_r.at[k], peer // SIDE, peer % SIDE
+        )
+
+    def finish(c):
+        j, h = c // PIECES, c % PIECES
+        s = lax.rem(place(a) - (j ^ (j >> 1)) + SIDE, SIDE)
+
+        @pl.loop(0, piece // STRIP)
+        def _(i):
+            r = pl.ds(pl.multiple_of(i * STRIP, STRIP), STRIP)
+            total = prec[c, r, :].astype(F32) + srec[c, r, :].astype(F32)
+            wr = pl.ds(pl.multiple_of(h * piece + i * STRIP, STRIP), STRIP)
+            packed = jnp.zeros(lane.shape, F32)
+            for m in range(queries):
+                got = jnp.sum(
+                    total * w[s, wr, m * span : (m + 1) * span], axis=1, keepdims=True
+                )
+                packed = jnp.where(lane == m, got, packed)
+            row = i * STRIP
+            at = pl.ds(pl.multiple_of(lax.rem(row, per), STRIP), STRIP)
+            sc[c * parcels + lax.div(row, per), at, :] = packed
+
+        for peer in range(c * parcels, (c + 1) * parcels):
+            k, copy = score(peer)
+
+            @pl.when(k == 0)
+            def _():
+                rsc[0] = sc[peer]
+
+            @pl.when(k > 0)
+            def _():
+                copy.start()
 
     dtiles = d_hbm.shape[1] // DROWS
 
@@ -312,71 +356,45 @@
     rotate_in()
     for c in (act_x, act_c, act_f):
         c.wait_send()
+    chain(0)
     damp(0, dtiles // 2)
     sum_across(0)
 
     ring(1).wait_recv()
     ring(2).start()
     rotate_out(1)
+    chain(1)
     damp(dtiles // 2, dtiles)
     sum_cores(1)
+    chain(2)
 
     ring(2).wait_recv()
     ring(3).start()
-    chain(0)
     rotate_out(2)
     sum_across(1)
-    chain(1)
-    contract(0)
+    chain(3)
+    contract(0, 2)
     sum_cores(2)
-    chain(2)
-    contract(1)
+    chain(4)
     sum_across(2)
-    chain(3)
+    chain(5)
 
     ring(3).wait_recv()
     rotate_out(3)
-    chain(4)
+    chain(6)
     sum_cores(3)
-    chain(5)
-    contract(2)
+    contract(2, 1)
+    chain(7)
     sum_across(3)
-    chain(6)
-    contract(3)
-    for step in range(7, chunks + last_a):
-        chain(step)
-
-    lane = lax.broadcasted_iota(jnp.int32, (STRIP, sc.shape[2]), 1)
-    per = sc.shape[1]
-    for s in range(SIDE):
-        for h in range(PIECES):
-            c = owner[s] * PIECES + h
-
-            @pl.loop(0, piece // STRIP)
-            def _(i):
-                r = pl.ds(pl.multiple_of(i * STRIP, STRIP), STRIP)
-                total = prec[c, r, :].astype(F32) + srec[c, r, :].astype(F32)
-                wr = pl.ds(pl.multiple_of(h * piece + i * STRIP, STRIP), STRIP)
-                packed = jnp.zeros(lane.shape, F32)
-                for m in range(queries):
-                    got = jnp.sum(
-                        total * w[s, wr, m * span : (m + 1) * span], axis=1, keepdims=True
-                    )
-                    packed = jnp.where(lane == m, got, packed)
-                row = owner[s] * rows + h * piece + i * STRIP
-                sc[row // per, pl.ds(pl.multiple_of(lax.rem(row, per), STRIP), STRIP), :] = packed
-
-    def score(k):
-        peer = lax.rem(me + k, SIDE * SIDE)
-        return remote(
-            sc.at[peer], rsc.at[k], sc_s.at[k], sc_r.at[k], peer // SIDE, lax.rem(peer, SIDE)
-        )
-
-    @pl.loop(1, others + 1)
-    def _(k):
-        score(k).start()
-
-    rsc[0] = sc[me]
+    chain(8)
+    contract(3, 1)
+    done = 0
+    for step in range(8, chunks + last_a):
+        if step > 8:
+            chain(step)
+        while done <= step - last_a:
+            finish(done)
+            done += 1
 
     for step in range(1, SIDE):
         ring(step).wait_send()
@@ -395,9 +413,12 @@
         def _():
             going_down(c).wait_send()
 
-    @pl.loop(1, others + 1)
-    def _(k):
-        score(k).wait()
+    for peer in range(SIDE * SIDE):
+        k, copy = score(peer)
+
+        @pl.when(k > 0)
+        def _():
+            copy.wait()
 
     total = rsc[0]
     for k in range(1, SIDE * SIDE):

time: 275 us -> 252 us (0.916)
  Pallas kernels: 272 us -> 249 us
    pallas_call x1, Pallas kernels: 272 us -> 249 us  [fused_scores(): pl.pallas_call(kernel, out_shape=(jax.ShapeDtypeStruct((per, 128), F32),...]
where the time goes in v2:
time: 252 us; the launch traced here: 250 us
  Pallas kernels  249 us (99%)
    pallas_call x1, Pallas kernels, fused_scores(): pl.pallas_call(kernel, out_shape=(jax.ShapeDtypeStruct((per, 128), F32),...  249 us

profile of v2, /device:TPU:0, one launch (start us, length us, event | category | flops | bytes accessed | tf_op | source)
XLA Modules:
  0.0 250.4 jit_solution(17652144548995194049)
XLA Ops:
  0.0 0.0 copy-start
  0.0 0.0 copy-start.1
  0.0 248.9 %shard_map.82 = (f32[48,128]{1,0:T(8,128)}, bf16[2,4096,2048]{2,1,0:T(8,128)(2,1)}) custom-call(bf16[192,2048]{1,0:T(8,128)(2,1)} %act_hbm.1, bf16[192,4096]{1,0:T(8,128)(2,1)} %og_hbm.1, bf16[2048,2048]{1,0:T(8,128)(2,1)} %ib_hbm.1, bf16[4096,4096]{1,0:T(8,128)(2,1)} %ob_hbm.1, bf16[4096,2048]{1,0:T(8,128)(2,1)} %eig_hbm.1, bf16[2,4096,2048]{2,1,0:T(8,128)(2,1)} %qg_hbm.1), custom_call_target="tpu_custom_call" | custom-call | flops 57982058496 | bytes 276824064 | tf_op jit(solution)/shard_map/pallas_call | solution.py:439
  248.9 0.0 copy-done.1
  248.9 0.1 select_reduce_fusion
  249.0 0.0 copy-done
  249.0 0.8 select_multiply_fusion
  249.8 0.6 copy.12
  (1 shorter events, 0.0 us)
Async XLA Ops:
  0.0 249.0 %copy-start = (s32[2]{0:T(128)S(1)}, s32[2]{0:T(128)}, u32[]{:S(2)}) copy-start(s32[2]{0:T(128)} %param.15) | copy-start | bytes 28
  0.0 248.9 %copy-start.1 = (s32[24]{0:T(128)S(1)}, s32[24]{0:T(128)}, u32[]{:S(2)}) copy-start(s32[24]{0:T(128)} %param.14) | copy-start | bytes 292

commit v3 on v2

--- a/solution.py
+++ b/solution.py
@@ -86,12 +86,21 @@
     act_c.start()
     ring(1).start()
 
-    def stream(count, source, view, compute):
+    tiles = span // TILE
+
+    def tile_copy(kind, k):
+        slot = lax.rem(k, 2)
+        if kind == "out":
+            source, view = ob_hbm.at[:, columns(k)], wbuf.at[slot]
+        elif kind == "in":
+            source, view = ib_hbm.at[:, columns(k)], wbuf.at[slot, pl.ds(0, span), :]
+        else:
+            source, view = d_hbm.at[k // tiles, :, columns(lax.rem(k, tiles))], wbuf.at[slot]
+        return pltpu.make_async_copy(source, view, wsem.at[slot])
+
+    def stream(kind, count, compute, ahead):
         def copy(k):
-            slot = lax.rem(k, 2)
-            return pltpu.make_async_copy(source(k), view(slot), wsem.at[slot])
-
-        copy(jnp.int32(0)).start()
+            return tile_copy(kind, k)
 
         @pl.loop(0, count)
         def _(k):
@@ -99,8 +108,14 @@
             def _():
                 copy(k + 1).start()
 
+            if ahead is not None:
+
+                @pl.when(k + 1 == count)
+                def _():
+                    tile_copy(ahead, jnp.int32(0)).start()
+
             copy(k).wait()
-            compute(k, view(lax.rem(k, 2)))
+            compute(k, wbuf.at[lax.rem(k, 2)])
 
     def columns(k):
         return pl.ds(pl.multiple_of(k * TILE, TILE), TILE)
@@ -123,12 +138,12 @@
     def whole_to_mate(s):
         return remote(ro.at[s, :, my_half], frecv.at[s], f_s.at[s], f_r.at[s], a, mate)
 
-    def rotate_out(s):
+    def rotate_out(s, ahead):
         def compute(k, tile):
             part = jnp.dot(og[s], tile[...], preferred_element_type=F32)
             ro[s, :, columns(k)] = part.astype(BF16)
 
-        stream(width // TILE, lambda k: ob_hbm.at[:, columns(k)], lambda v: wbuf.at[v], compute)
+        stream("out", width // TILE, compute, ahead)
         to_mate(s).start()
 
     def sum_cores(s):
@@ -153,19 +168,18 @@
         strips(rows, body)
         whole_to_mate(s).start()
 
-    def rotate_in():
+    def rotate_in(ahead):
         def compute(k, tile):
             for s in range(SIDE):
-                part = jnp.dot(act[s], tile[...], preferred_element_type=F32).astype(BF16)
+                part = jnp.dot(
+                    act[s], tile[pl.ds(0, span), :], preferred_element_type=F32
+                ).astype(BF16)
                 for h in range(PIECES):
                     rip[act_owner[s] * PIECES + h, :, columns(k)] = part[
                         h * piece : (h + 1) * piece
                     ]
 
-        stream(
-            span // TILE, lambda k: ib_hbm.at[:, columns(k)],
-            lambda v: wbuf.at[v, pl.ds(0, span), :], compute,
-        )
+        stream("in", span // TILE, compute, ahead)
 
     def damp(first, last):
         def block(k):
@@ -212,9 +226,7 @@
         for k in (last - 2, last - 1):
             store(jnp.int32(k)).wait()
 
-    tiles = span // TILE
-
-    def contract(s, count):
+    def contract(s, count, ahead):
         for k in range(s, s + count):
             whole_to_mate(k).wait_recv()
         slots = pl.ds(s, count)
@@ -226,11 +238,7 @@
             got = got + jnp.dot(theirs, tile[other_rows, :], preferred_element_type=F32)
             w[slots, :, columns(k)] = got.reshape(count, rows, TILE)
 
-        stream(
-            queries * tiles,
-            lambda k: d_hbm.at[k // tiles, :, columns(lax.rem(k, tiles))],
-            lambda v: wbuf.at[v], compute,
-        )
+        stream("damped", queries * tiles, compute, ahead)
 
     last_a = SIDE - 1
     up = lax.rem(a + 1, SIDE)
@@ -345,15 +353,16 @@
 
     dtiles = d_hbm.shape[1] // DROWS
 
+    tile_copy("out", jnp.int32(0)).start()
     own_og.wait()
-    rotate_out(0)
+    rotate_out(0, "in")
     own_act.wait()
     act_x.wait_recv()
     act_f.start()
     act_c.wait_recv()
     sum_cores(0)
     act_f.wait_recv()
-    rotate_in()
+    rotate_in("out")
     for c in (act_x, act_c, act_f):
         c.wait_send()
     chain(0)
@@ -362,7 +371,7 @@
 
     ring(1).wait_recv()
     ring(2).start()
-    rotate_out(1)
+    rotate_out(1, "out")
     chain(1)
     damp(dtiles // 2, dtiles)
     sum_cores(1)
@@ -370,24 +379,24 @@
 
     ring(2).wait_recv()
     ring(3).start()
-    rotate_out(2)
+    rotate_out(2, "damped")
     sum_across(1)
     chain(3)
-    contract(0, 2)
+    contract(0, 2, "out")
     sum_cores(2)
     chain(4)
     sum_across(2)
     chain(5)
 
     ring(3).wait_recv()
-    rotate_out(3)
+    rotate_out(3, "damped")
     chain(6)
     sum_cores(3)
-    contract(2, 1)
+    contract(2, 1, "damped")
     chain(7)
     sum_across(3)
     chain(8)
-    contract(3, 1)
+    contract(3, 1, None)
     done = 0
     for step in range(8, chunks + last_a):
         if step > 8:

time: 252 us -> 243 us (0.964); the launches traced: 250 us -> 239 us
  Pallas kernels: 249 us -> 237 us
    pallas_call x1, Pallas kernels: 249 us -> 237 us  [fused_scores(): pl.pallas_call(kernel, out_shape=(jax.ShapeDtypeStruct((per, 128), F32),...]
where the time goes in v3:
time: 243 us; the launch traced here: 239 us
  Pallas kernels  237 us (98%)
    pallas_call x1, Pallas kernels, fused_scores(): pl.pallas_call(kernel, out_shape=(jax.ShapeDtypeStruct((per, 128), F32),...  237 us

profile of v3, /device:TPU:0, one launch (start us, length us, event | category | flops | bytes accessed | tf_op | source)
XLA Modules:
  0.0 238.6 jit_solution(10402435224980468300)
XLA Ops:
  0.0 0.0 copy-start
  0.0 0.0 copy-start.1
  0.0 237.1 %shard_map.82 = (f32[48,128]{1,0:T(8,128)}, bf16[2,4096,2048]{2,1,0:T(8,128)(2,1)}) custom-call(bf16[192,2048]{1,0:T(8,128)(2,1)} %act_hbm.1, bf16[192,4096]{1,0:T(8,128)(2,1)} %og_hbm.1, bf16[2048,2048]{1,0:T(8,128)(2,1)} %ib_hbm.1, bf16[4096,4096]{1,0:T(8,128)(2,1)} %ob_hbm.1, bf16[4096,2048]{1,0:T(8,128)(2,1)} %eig_hbm.1, bf16[2,4096,2048]{2,1,0:T(8,128)(2,1)} %qg_hbm.1), custom_call_target="tpu_custom_call" | custom-call | flops 57982058496 | bytes 276824064 | tf_op jit(solution)/shard_map/pallas_call | solution.py:448
  237.1 0.0 copy-done.1
  237.1 0.1 select_reduce_fusion
  237.2 0.0 copy-done
  237.2 0.8 select_multiply_fusion
  238.0 0.6 copy.12
  (1 shorter events, 0.0 us)
Async XLA Ops:
  0.0 237.2 %copy-start = (s32[2]{0:T(128)S(1)}, s32[2]{0:T(128)}, u32[]{:S(2)}) copy-start(s32[2]{0:T(128)} %param.15) | copy-start | bytes 28
  0.0 237.1 %copy-start.1 = (s32[24]{0:T(128)S(1)}, s32[24]{0:T(128)}, u32[]{:S(2)}) copy-start(s32[24]{0:T(128)} %param.14) | copy-start | bytes 292
